TPU v7x, 32 devices: a whole 2x2x4 slice. The times are simulated.
32 devices in a mesh: groups: 1, cells: 32 (over z, y, x, core).
Axes of the slice: x: 2, y: 2, z: 4, core: 2. Of those that a mesh axis runs over, the one named last changes fastest.
Arguments:
- expression: bfloat16 [49152, 3072], P(('groups', 'cells')), may hold values from 0.019897461 to 4
- dataset_ids: int32 [49152, 1], P(('groups', 'cells')), may hold values from 0 to 31; in each aligned block of 1536 rows (0 to 1535, 1536 to 3071, ...) at most 64 rows name the same one
- owner_map: int32 [32], P('groups'), may hold values from 0 to 31, each once
- atlas_sizes: int32 [32], P('groups'), may hold values from 16384 to 131071
- loadings: bfloat16 [64, 49152], P(None, ('groups', 'cells')), may hold values from 0.049804688 to 1
- shared: float32 [64, 3072], P('groups'), may hold values from 0 to 0.5
- specific: float32 [32, 64, 3072], P(('groups', 'cells')), may hold values from 0 to 0.2
Outputs:
- loadings_out: float32 [64, 49152], P(None, ('groups', 'cells'))
- shared_out: float32 [64, 3072], P('groups')
- specific_out: float32 [32, 64, 3072], P(('groups', 'cells'))
Inputs may be any that keep to these rules, and one draw needn't show every extreme that they name: `dataset_ids`: among the cells of one device at most 64 belong to one dataset, and exactly 64 do in some dataset; every dataset has cells in the window. `owner_map`: each device owns exactly one dataset.
All inputs are finite; a program needn't handle non-finite values. Where the computation divides by a largest or mean magnitude, that divisor is 1e-20 or more.
Results may differ from a plain program's by a relative error of at most 0.0003.
Values may be sent and summed in bfloat16 or wider, within the bound.
A program may use at most 192 MiB of HBM per device.

v0:
```python
import jax
import jax.numpy as jnp
from jax import lax
from jax.sharding import PartitionSpec as P

GENES = 3072
FACTORS = 64
SLOTS = 64
PASSES = 3


penalty = 5.0


def hdot(left, right):
    return jnp.dot(left, right, preferred_element_type=jnp.float32, precision=lax.Precision.HIGHEST)


def refine(rows, start_load, factor_low, curvature, step_size):
    projected = jnp.einsum("kg,nsg->nsk", factor_low, rows, preferred_element_type=jnp.float32)
    loading = start_load.astype(jnp.float32)
    for turn in range(PASSES):
        applied = jnp.einsum(
            "jk,nsj->nsk",
            curvature,
            loading,
            preferred_element_type=jnp.float32,
            precision=lax.Precision.HIGHEST,
        )
        loading = jnp.maximum(loading - step_size * (applied - projected), 0.0)
    return loading


def body(expression, dataset_ids, owner_map, atlas_sizes, loadings, shared, specific):
    dataset_of = dataset_ids[:, 0]
    device_count = lax.axis_size("cells")
    dataset_count = owner_map.shape[0]
    chosen = (dataset_of[:, None] == jnp.arange(dataset_count, dtype=jnp.int32)[None, :]).astype(
        jnp.int32
    )
    target = jnp.sum(chosen * owner_map[None, :], axis=1)
    target_hot = (target[:, None] == jnp.arange(device_count, dtype=jnp.int32)[None, :]).astype(
        jnp.int32
    )
    slot_index = jnp.sum((jnp.cumsum(target_hot, axis=0) - target_hot) * target_hot, axis=1)
    send_rows = (
        jnp.zeros((device_count, SLOTS, GENES), jnp.bfloat16).at[target, slot_index].set(expression)
    )
    send_load = (
        jnp.zeros((device_count, SLOTS, FACTORS), jnp.bfloat16)
        .at[target, slot_index]
        .set(loadings.T)
    )
    send_flag = jnp.zeros((device_count, SLOTS), jnp.bfloat16).at[target, slot_index].set(1.0)
    owner = lax.axis_index("cells")
    own_specific = specific[0]
    factor = shared + own_specific
    factor_low = factor.astype(jnp.bfloat16)
    curvature = hdot(factor, factor.T) + penalty * hdot(own_specific, own_specific.T)
    step_size = 1.0 / jnp.max(jnp.sum(jnp.abs(curvature), axis=1))
    recv_rows, recv_load, recv_flag = (
        lax.all_to_all(send_rows, "cells", split_axis=0, concat_axis=0, tiled=True),
        lax.all_to_all(send_load, "cells", split_axis=0, concat_axis=0, tiled=True),
        lax.all_to_all(send_flag, "cells", split_axis=0, concat_axis=0, tiled=True),
    )
    loading = refine(recv_rows, recv_load, factor_low, curvature, step_size)
    count = jnp.sum(recv_flag.astype(jnp.float32))
    gram_stat = (
        jnp.einsum(
            "nsk,nsj->kj",
            loading,
            loading,
            preferred_element_type=jnp.float32,
            precision=lax.Precision.HIGHEST,
        )
        / count
    )
    cross_stat = (
        jnp.einsum(
            "nsk,nsg->kg",
            loading.astype(jnp.bfloat16),
            recv_rows,
            preferred_element_type=jnp.float32,
        )
        / count
    )
    weight_own = (
        jnp.sum(jnp.where(owner_map == owner, atlas_sizes, 0)).astype(jnp.float32) / 65536.0
    )
    gradient = hdot(gram_stat, factor) - cross_stat
    row_bound = jnp.max(jnp.sum(gram_stat, axis=1))
    new_specific = jnp.maximum(
        own_specific
        - (gradient + penalty * hdot(gram_stat, own_specific))
        / ((1.0 + penalty) * row_bound + 1e-06),
        0.0,
    )
    returned = lax.all_to_all(loading, "cells", split_axis=0, concat_axis=0, tiled=True)
    loadings_out = returned[target, slot_index].T
    grad_term = weight_own * gradient
    bound_term = weight_own * row_bound
    grad_total, bound_total = lax.psum((grad_term, bound_term), "cells")
    shared_out = jnp.maximum(shared - grad_total / bound_total, 0.0)
    return (loadings_out, shared_out, new_specific[None])


def solution(mesh):
    placed = (
        P(("groups", "cells"), None),
        P(("groups", "cells"), None),
        P("groups"),
        P("groups"),
        P(None, ("groups", "cells")),
        P("groups", None),
        P(("groups", "cells"), None, None),
    )
    return jax.shard_map(
        body,
        mesh=mesh,
        in_specs=placed,
        out_specs=(
            P(None, ("groups", "cells")),
            P("groups", None),
            P(("groups", "cells"), None, None),
        ),
        check_vma=False,
    )
```

profile of v0, /device:TPU:0, one launch (start us, length us, event | category | flops | bytes accessed | tf_op | source)
XLA Modules:
  0.0 530.2 jit_solution(3536061806633543873)
XLA Ops:
  7.2 0.7 reduce.7
  7.9 0.8 select_reduce_fusion
  8.7 9.1 %reduce-window.6 = s32[32,12,128]{2,1,0:T(8,128)S(1)} reduce-window(s32[32,12,128]{2,1,0:T(8,128)S(1)} %fusion.27, s32[]{:T(128)} %constant.14.clone.1), window={size=1x1x128 pad=0_0x0_0x127_0}, to_apply=%region_1.0 | reduce-window | flops 6242304 | bytes 393220 | tf_op jit(solution)/shard_map/reduce-window
  18.5 0.7 multiply_reduce_fusion
  19.2 0.8 and_reduce_fusion
  20.0 11.1 %scatter_custom_fusion.2 = bf16[2048]{0:T(1024)(128)(2,1)S(1)} fusion(s32[1536]{0:T(1024)S(1)} %broadcast_select_fusion, bf16[1536]{0:T(1024)(128)(2,1)S(1)} %broadcast.105, bf16[]{:T(256)} %constant.13.clone.1), kind=kCustom, calls=%fused_computation.64 | custom fusion | bytes 4098
  31.1 0.7 all_to_all.20
  31.8 7.3 %all-to-all-start.3 = ((bf16[32,1,64]{2,1,0:T(2,128)(2,1)}), bf16[32,1,64]{2,1,0:T(2,128)(2,1)S(1)}, u32[]{:S(2)}, u32[]{:S(2)}) async-start(bf16[32,1,64]{2,1,0:T(2,128)(2,1)} %all_to_all.20), calls=%async_computation.3 | async-start | bytes 32768 | tf_op jit(solution)/shard_map/all_to_all | solution.py:64
  39.1 1.1 copy.28
  40.3 4.6 scatter_custom_fusion
  44.9 1.1 reshape.104
  46.2 5.8 %all-to-all-start = ((bf16[32,2,2048]{2,1,0:T(2,128)(2,1)}), bf16[32,2,2048]{2,1,0:T(2,128)(2,1)S(1)}, u32[]{:S(2)}, u32[]{:S(2)}) async-start(bf16[32,2,2048]{2,1,0:T(2,128)(2,1)} %reshape.104), calls=%async_computation | async-start | bytes 524288 | tf_op jit(solution)/shard_map/all_to_all | solution.py:63
  52.0 21.0 %scatter_custom_fusion.1 = bf16[2048,3072]{1,0:T(8,128)(2,1)} fusion(s32[1536]{0:T(1024)S(1)} %broadcast_select_fusion, bf16[1536,3072]{1,0:T(8,128)(2,1)} %param.7, bf16[]{:T(256)} %constant.13.clone.1), kind=kCustom, calls=%fused_computation.4 | custom fusion | bytes 12583424
  73.0 5.8 %all-to-all-start.1 = ((bf16[32,64,3072]{2,1,0:T(8,128)(2,1)}), bf16[32,64,3072]{2,1,0:T(8,128)(2,1)}, u32[]{:S(2)}, u32[]{:S(2)}) async-start(bf16[32,64,3072]{2,1,0:T(8,128)(2,1)} %bitcast.70), calls=%async_computation.1 | async-start | bytes 25165824 | tf_op jit(solution)/shard_map/all_to_all | solution.py:62
  80.4 0.8 fusion.37
  81.2 0.8 abs_reduce_fusion
  84.3 273.3 %all-to-all-done.1 = bf16[32,64,3072]{2,1,0:T(8,128)(2,1)} async-done(((bf16[32,64,3072]{2,1,0:T(8,128)(2,1)}), bf16[32,64,3072]{2,1,0:T(8,128)(2,1)}, u32[]{:S(2)}, u32[]{:S(2)}) %all-to-all-start.1) | async-done | bytes 12582944 | tf_op jit(solution)/shard_map/all_to_all | solution.py:62
  357.5 6.5 %fusion.22 = f32[32,64,64]{2,1,0:T(8,128)S(1)} fusion(bf16[32,64,3072]{2,1,0:T(8,128)(2,1)} %all-to-all-done.1, f32[64,3072]{1,0:T(8,128)S(1)} %copy-done, f32[1,64,3072]{2,1,0:T(8,128)S(1)} %copy-done.1), kind=kOutput, calls=%fused_computation.36 | convolution fusion | flops 805699584 | bytes 14680064 | tf_op jit(solution)/shard_map/kg,nsg->nsk/dot_general | solution.py:20
  364.6 1.0 fusion.12
  365.7 1.1 fusion.13
  366.8 2.6 fusion.38
  369.3 7.6 %fusion.3 = f32[64,3072]{1,0:T(8,128)S(1)} fusion(bf16[32,64,3072]{2,1,0:T(8,128)(2,1)} %all-to-all-done.1, f32[32,64,64]{2,1,0:T(8,128)S(1)} %fusion.13, f32[]{:T(128)} %convert_reduce_fusion), kind=kOutput, calls=%fused_computation.10 | convolution fusion | flops 805634048 | bytes 13893636 | tf_op jit(solution)/shard_map/nsk,nsg->kg/dot_general | solution.py:79
  376.9 1.7 broadcast_multiply_fusion
  378.7 1.5 reshape.106
  380.2 2.6 all-to-all-start.2
  384.0 40.9 %psum.15 = f32[]{:T(128)} all-reduce(f32[]{:T(128)S(6)} %mul.57), channel_id=1, replica_groups=mesh['groups'=1,'cells'=32] {'cells'}, use_global_device_ids=true, to_apply=%region_14.15 | all-reduce | flops 1 | bytes 8 | tf_op jit(solution)/shard_map/psum | solution.py:102
  425.6 1.8 fusion.7
  427.4 79.3 %all-reduce.2.cloned.1.call-done = f32[64,3072]{1,0:T(8,128)} async-done(((f32[64,3072]{1,0:T(8,128)}), f32[64,3072]{1,0:T(8,128)}) %all-reduce.2.cloned.1.call-update) | async-done | bytes 786448 | tf_op jit(solution)/shard_map/psum | solution.py:102
  506.8 2.8 subtract_maximum_fusion
  510.1 1.9 reduce.12
  512.5 9.9 %gather_fusion = f32[1536,64]{1,0:T(8,128)S(1)} fusion(f32[32,64,64]{2,1,0:T(8,128)S(1)} %reshape.107, s32[1536]{0:T(1024)S(1)} %get-tuple-element.12), kind=kCustom, calls=%fused_computation | custom fusion | bytes 798720 | tf_op jit(solution)/shard_map/gather | solution.py:99
  522.4 1.0 copy.35
  (31 shorter events, 5.6 us)
Async XLA Ops:
  31.8 14.4 %all-to-all-start.3 = ((bf16[32,1,64]{2,1,0:T(2,128)(2,1)}), bf16[32,1,64]{2,1,0:T(2,128)(2,1)S(1)}, u32[]{:S(2)}, u32[]{:S(2)}) async-start(bf16[32,1,64]{2,1,0:T(2,128)(2,1)} %all_to_all.20), calls=%async_computation.3 | async-start | bytes 32768 | tf_op jit(solution)/shard_map/all_to_all | solution.py:64
  46.2 26.8 %all-to-all-start = ((bf16[32,2,2048]{2,1,0:T(2,128)(2,1)}), bf16[32,2,2048]{2,1,0:T(2,128)(2,1)S(1)}, u32[]{:S(2)}, u32[]{:S(2)}) async-start(bf16[32,2,2048]{2,1,0:T(2,128)(2,1)} %reshape.104), calls=%async_computation | async-start | bytes 524288 | tf_op jit(solution)/shard_map/all_to_all | solution.py:63
  73.0 6.1 %copy-start.2 = (s32[32]{0:T(128)S(1)}, s32[32]{0:T(128)}, u32[]{:S(2)}) copy-start(s32[32]{0:T(128)} %param.9) | copy-start | bytes 388
  73.0 6.1 %copy-start.3 = (s32[32]{0:T(128)S(1)}, s32[32]{0:T(128)}, u32[]{:S(2)}) copy-start(s32[32]{0:T(128)} %param.10) | copy-start | bytes 388
  73.0 7.4 %copy-start = (f32[64,3072]{1,0:T(8,128)S(1)}, f32[64,3072]{1,0:T(8,128)}, u32[]{:S(2)}) copy-start(f32[64,3072]{1,0:T(8,128)} %param.12) | copy-start | bytes 2359300
  73.0 7.4 %copy-start.1 = (f32[1,64,3072]{2,1,0:T(8,128)S(1)}, f32[1,64,3072]{2,1,0:T(8,128)}, u32[]{:S(2)}) copy-start(f32[1,64,3072]{2,1,0:T(8,128)} %param.13) | copy-start | bytes 2359300
  73.0 284.5 %all-to-all-start.1 = ((bf16[32,64,3072]{2,1,0:T(8,128)(2,1)}), bf16[32,64,3072]{2,1,0:T(8,128)(2,1)}, u32[]{:S(2)}, u32[]{:S(2)}) async-start(bf16[32,64,3072]{2,1,0:T(8,128)(2,1)} %bitcast.70), calls=%async_computation.1 | async-start | bytes 25165824 | tf_op jit(solution)/shard_map/all_to_all | solution.py:62
  78.8 428.0 %all-reduce.2.cloned.1.call-start = ((), (), s32[]{:S(2)}) async-start(), calls=%async_computation.4 | async-start | bytes 1572864 | tf_op jit(solution)/shard_map/psum | solution.py:102
  380.2 129.4 %all-to-all-start.2 = ((f32[32,1,4096]{2,1,0:T(1,128)}), f32[32,1,4096]{2,1,0:T(1,128)S(1)}, u32[]{:S(2)}, u32[]{:S(2)}) async-start(f32[32,1,4096]{2,1,0:T(1,128)} %reshape.106), calls=%async_computation.2 | async-start | bytes 1048576 | tf_op jit(solution)/shard_map/all_to_all | solution.py:98
Sparse Core Ops, SparseCore 0:
  378.8 127.9 all-reduce.1
where the time goes:
time: 531 us; the launch traced here: 530 us
  waiting for transfers between devices  353 us (66%)
  local copies, waits for them, and re-layouts  53.7 us (10%)
  blocking collectives  40.9 us (8%)
  matrix products  24.5 us (5%)
  starting transfers between devices  21.8 us (4%)
  other arithmetic  19.6 us (4%)
  between operations  16.9 us (3%)
    all_to_all x1, waiting for transfers between devices, body(): lax.all_to_all(send_rows, 'cells', split_axis=0, concat_axis=0, tiled=True)  273 us
    psum x1, waiting for transfers between devices, body(): grad_total, bound_total = lax.psum((grad_term, bound_term), 'cells')  79.3 us
    unnamed x17, local copies, waits for them, and re-layouts  41 us
    psum x1, blocking collectives, body(): grad_total, bound_total = lax.psum((grad_term, bound_term), 'cells')  40.9 us
  transfers between devices with their start and end apart: 5, of which 3 were waited for; matrix products, arithmetic and copies ran while one was open for 7% of the time, Pallas kernels for 0%

commit v1 on v0

v1 whole, which is shorter than its diff:
```python
import jax
import jax.numpy as jnp
from jax import lax
from jax.sharding import PartitionSpec as P

PASSES = 3
PENALTY = 5.0


def hdot(left, right):
    return jnp.dot(left, right, preferred_element_type=jnp.float32, precision=lax.Precision.HIGHEST)


def split(x):
    high = lax.reduce_precision(x, 8, 7)
    return high.astype(jnp.bfloat16), (x - high).astype(jnp.bfloat16)


def body(expression, dataset_ids, owner_map, atlas_sizes, loadings, shared, specific):
    owners = lax.axis_size("cells")
    me = lax.axis_index("cells")
    cells, genes = expression.shape
    factors = shared.shape[0]
    v = specific[0]
    q = shared + v
    qb_all = lax.all_gather(q.astype(jnp.bfloat16), "cells", axis=0, tiled=True)
    curvature = hdot(q, q.T) + PENALTY * hdot(v, v.T)
    step = 1.0 / jnp.max(jnp.sum(jnp.abs(curvature), axis=1))
    small = jnp.concatenate([curvature * step, jnp.full((factors, factors), step)], axis=1)
    small_all = lax.all_gather(small, "cells", axis=0, tiled=True)
    ids = dataset_ids[:, 0]
    chosen = ids[:, None] == jnp.arange(owner_map.shape[0], dtype=jnp.int32)[None, :]
    target = jnp.sum(jnp.where(chosen, owner_map[None, :], 0), axis=1)
    mask = target[None, :] == jnp.arange(owners, dtype=jnp.int32)[:, None]
    count_all = lax.psum(jnp.sum(mask.astype(jnp.float32), axis=1), "cells")

    def pick(stacked):
        return jnp.sum(
            jnp.where(mask[:, None, :], stacked.reshape(owners, factors, cells), 0.0), axis=0
        )

    m_high, m_low = split(small_all[:, :factors])
    m_cat = jnp.concatenate([m_high, m_low, m_high], axis=1)
    steps = small_all.reshape(owners, factors, 2 * factors)[:, 0, factors]
    cell_step = jnp.sum(jnp.where(mask, steps[:, None], 0.0), axis=0)
    projected = pick(
        lax.dot_general(
            qb_all, expression, (((1,), (1,)), ((), ())), preferred_element_type=jnp.float32
        )
    )
    pull = projected * cell_step[None, :]
    h = loadings.astype(jnp.float32)
    for _ in range(PASSES):
        high, low = split(h)
        h_cat = jnp.concatenate([high, high, low], axis=0)
        applied = pick(jnp.dot(m_cat, h_cat, preferred_element_type=jnp.float32))
        h = jnp.maximum(h - applied + pull, 0.0)
    high, low = split(h)
    masked = jnp.where(mask[:, None, :], high[None], jnp.bfloat16(0)).reshape(
        owners * factors, cells
    )
    gram_part = jnp.dot(
        masked, jnp.concatenate([high.T, low.T], axis=1), preferred_element_type=jnp.float32
    )
    cross_part = jnp.dot(masked, expression, preferred_element_type=jnp.float32)
    gram2 = lax.psum_scatter(gram_part, "cells", scatter_dimension=0, tiled=True)
    cross = lax.psum_scatter(cross_part, "cells", scatter_dimension=0, tiled=True)
    count = jnp.sum(jnp.where(jnp.arange(owners) == me, count_all, 0.0))
    mixed = gram2[:, factors:]
    gram = (gram2[:, :factors] + mixed + mixed.T) / count
    weight = jnp.sum(jnp.where(owner_map == me, atlas_sizes, 0)).astype(jnp.float32) / 65536.0
    gradient = hdot(gram, q) - cross / count
    bound = jnp.max(jnp.sum(gram, axis=1))
    new_specific = jnp.maximum(
        v - (gradient + PENALTY * hdot(gram, v)) / ((1.0 + PENALTY) * bound + 1e-06), 0.0
    )
    grad_total, bound_total = lax.psum((weight * gradient, weight * bound), "cells")
    shared_out = jnp.maximum(shared - grad_total / bound_total, 0.0)
    return (h, shared_out, new_specific[None])


def solution(mesh):
    placed = (
        P(("groups", "cells"), None),
        P(("groups", "cells"), None),
        P("groups"),
        P("groups"),
        P(None, ("groups", "cells")),
        P("groups", None),
        P(("groups", "cells"), None, None),
    )
    return jax.shard_map(
        body,
        mesh=mesh,
        in_specs=placed,
        out_specs=(
            P(None, ("groups", "cells")),
            P("groups", None),
            P(("groups", "cells"), None, None),
        ),
        check_vma=False,
    )
```

time: 531 us -> 746 us (1.40)
  waiting for transfers between devices: 353 us -> 539 us
  matrix products: 24.5 us -> 79.4 us
  local copies, waits for them, and re-layouts: 53.7 us -> 3.35 us
  blocking collectives: 40.9 us -> 79.2 us
  starting transfers between devices: 21.8 us -> 0.21 us
  other arithmetic: 19.6 us -> 27.2 us
    reduce_scatter x0 -> x2, waiting for transfers between devices: none -> 312 us  [the longest x1 246 us: body(): lax.psum_scatter(cross_part, 'cells', scatter_dimension=0, tiled=True)]
    all_to_all x4 -> x0, waiting for transfers between devices: 273 us -> none  [the longest x1 273 us: body(): lax.all_to_all(send_rows, 'cells', split_axis=0, concat_axis=0, tiled=True)]
    all_gather x0 -> x2, waiting for transfers between devices: none -> 141 us  [the longest x1 89.3 us: body(): qb_all = lax.all_gather(q.astype(jnp.bfloat16), 'cells', axis=0, tiled=True)]
    dot_general x6, matrix products: 19.4 us -> 69.1 us  [the longest x1 26.7 us: body(): cross_part = jnp.dot(masked, expression, preferred_element_type=jnp.float32)]
    unnamed x17 -> x16, local copies, waits for them, and re-layouts: 41 us -> 0.75 us
    psum x1 -> x2, blocking collectives: 40.9 us -> 79.2 us  [the longest x1 40.5 us: body(): lax.psum((weight * gradient, weight * bound), 'cells')]
    all_to_all x4 -> x0, starting transfers between devices: 21.5 us -> none  [the longest x1 7.3 us: body(): lax.all_to_all(send_flag, 'cells', split_axis=0, concat_axis=0, tiled=True)]
    reduce_sum x4 -> x8, other arithmetic: 2.11 us -> 14.3 us  [the longest x3 10.7 us: pick(): jnp.sum(jnp.where(mask[:, None, :], stacked.reshape(owners, factors, cell...]
  transfers between devices with their start and end apart: 5 -> 5, of which waited for: 3 -> 5; matrix products, arithmetic and copies ran while one was open for 7% -> 6% of each run, Pallas kernels for 0% -> 0%
where the time goes in v1:
time: 746 us; the launch traced here: 745 us
  waiting for transfers between devices  539 us (72%)
  matrix products  79.4 us (11%)
  blocking collectives  79.2 us (11%)
  other arithmetic  27.2 us (4%)
  between operations  16.6 us (2%)
    reduce_scatter x1, waiting for transfers between devices, body(): lax.psum_scatter(cross_part, 'cells', scatter_dimension=0, tiled=True)  246 us
    all_gather x1, waiting for transfers between devices, body(): qb_all = lax.all_gather(q.astype(jnp.bfloat16), 'cells', axis=0, tiled=True)  89.3 us
    psum x1, waiting for transfers between devices, body(): lax.psum((weight * gradient, weight * bound), 'cells')  86.7 us
    reduce_scatter x1, waiting for transfers between devices, body(): lax.psum_scatter(gram_part, 'cells', scatter_dimension=0, tiled=True)  65.2 us
    all_gather x1, waiting for transfers between devices, body(): small_all = lax.all_gather(small, 'cells', axis=0, tiled=True)  51.7 us
    psum x1, blocking collectives, body(): lax.psum((weight * gradient, weight * bound), 'cells')  40.5 us
    psum x1, blocking collectives, body(): count_all = lax.psum(jnp.sum(mask.astype(jnp.float32), axis=1), 'cells')  38.7 us
    dot_general x1, matrix products, body(): cross_part = jnp.dot(masked, expression, preferred_element_type=jnp.float32)  26.7 us
  transfers between devices with their start and end apart: 5, of which 5 were waited for; matrix products, arithmetic and copies ran while one was open for 6% of the time, Pallas kernels for 0%

profile of v1, /device:TPU:0, one launch (start us, length us, event | category | flops | bytes accessed | tf_op | source)
XLA Modules:
  0.0 745.3 jit_solution(15185952283999684537)
XLA Ops:
  7.2 2.7 fusion.47
  9.9 2.2 abs_reduce_fusion
  13.5 0.6 concatenate.18
  14.2 2.2 fusion.46
  16.4 0.7 reduce
  17.2 0.8 select_reduce_fusion.5
  18.0 1.0 fusion.27
  18.9 51.7 %all-gather.3.cloned.1.call-done = f32[2048,128]{1,0:T(8,128)} async-done(((f32[64,128]{1,0:T(8,128)}), f32[2048,128]{1,0:T(8,128)}) %all-gather.3.cloned.1.call-update) | async-done | bytes 1048592 | tf_op jit(solution)/shard_map/all_gather | solution.py:30
  70.6 1.0 slice.17
  71.9 1.4 fusion.6
  73.3 6.5 fusion.9
  79.7 89.3 %all-gather.5.cloned.1.call-done = bf16[2048,3072]{1,0:T(8,128)(2,1)} async-done(((bf16[64,3072]{1,0:T(8,128)(2,1)}), bf16[2048,3072]{1,0:T(8,128)(2,1)}) %all-gather.5.cloned.1.call-update) | async-done | bytes 12582928 | tf_op jit(solution)/shard_map/all_gather | solution.py:26
  169.1 26.7 %fusion.52 = f32[2048,1536]{1,0:T(8,128)} fusion(bf16[2048,3072]{1,0:T(8,128)(2,1)} %all-gather.5.cloned.1.call-done, bf16[1536,3072]{1,0:T(8,128)(2,1)} %param.7), kind=kOutput, calls=%fused_computation.85 | convolution fusion | flops 19327352832 | bytes 34603008 | tf_op jit(solution)/shard_map/dot_general | solution.py:47
  195.8 6.9 select_reduce_fusion.2
  202.9 1.9 fusion.15
  204.7 1.9 select_reduce_fusion.1
  206.7 1.9 fusion.21
  208.6 1.9 select_reduce_fusion
  210.6 3.2 broadcast_select_fusion
  213.9 5.6 fusion.34
  219.5 26.7 %fusion.53 = f32[2048,3072]{1,0:T(8,128)} fusion(bf16[2048,1536]{1,0:T(8,128)(2,1)} %bitcast.7, bf16[1536,3072]{1,0:T(8,128)(2,1)} %param.7), kind=kOutput, calls=%fused_computation.86 | convolution fusion | flops 19327352832 | bytes 40894464 | tf_op jit(solution)/shard_map/dot_general | solution.py:65
  246.9 0.6 fusion.40
  248.2 38.7 %psum.21 = f32[32]{0:T(128)S(1)} all-reduce(f32[32]{0:T(128)S(1)} %get-tuple-element.5), channel_id=1, replica_groups=mesh['groups'=1,'cells'=32] {'cells'}, use_global_device_ids=true, to_apply=%region_11.12 | all-reduce | flops 32 | bytes 256 | tf_op jit(solution)/shard_map/psum | solution.py:35
  287.5 65.2 %reduce-scatter.3.cloned.1.call-done = f32[64,128]{1,0:T(8,128)} async-done(((f32[2048,128]{1,0:T(8,128)}), f32[64,128]{1,0:T(8,128)}) %reduce-scatter.3.cloned.1.call-update) | async-done | bytes 32784 | tf_op jit(solution)/shard_map/reduce_scatter | solution.py:66
  352.7 0.9 fusion.51
  353.8 1.5 fusion.48
  355.3 246.3 %reduce-scatter.5.cloned.1.call-done = f32[64,3072]{1,0:T(8,128)} async-done(((f32[2048,3072]{1,0:T(8,128)}), f32[64,3072]{1,0:T(8,128)}) %reduce-scatter.5.cloned.1.call-update) | async-done | bytes 786448 | tf_op jit(solution)/shard_map/reduce_scatter | solution.py:67
  601.6 3.5 broadcast_multiply_fusion
  606.4 40.5 %psum.23 = f32[]{:T(128)} all-reduce(f32[]{:T(128)S(6)} %mul.43), channel_id=1, replica_groups=mesh['groups'=1,'cells'=32] {'cells'}, use_global_device_ids=true, to_apply=%region_17.18 | all-reduce | flops 1 | bytes 8 | tf_op jit(solution)/shard_map/psum | solution.py:77
  647.5 1.8 fusion.4
  649.3 86.7 %all-reduce.3.cloned.1.call-done = f32[64,3072]{1,0:T(8,128)} async-done(((f32[64,3072]{1,0:T(8,128)}), f32[64,3072]{1,0:T(8,128)}) %all-reduce.3.cloned.1.call-update) | async-done | bytes 786448 | tf_op jit(solution)/shard_map/psum | solution.py:77
  736.0 2.7 subtract_maximum_fusion
  (40 shorter events, 3.5 us)
Async XLA Ops:
  7.2 63.5 %all-gather.3.cloned.1.call-start = ((), (), s32[]{:S(2)}) async-start(), calls=%async_computation.2 | async-start | bytes 1081344 | tf_op jit(solution)/shard_map/all_gather | solution.py:30
  14.1 154.9 %all-gather.5.cloned.1.call-start = ((), (), s32[]{:S(2)}) async-start(), calls=%async_computation.3 | async-start | bytes 12976128 | tf_op jit(solution)/shard_map/all_gather | solution.py:26
  16.4 336.3 %reduce-scatter.3.cloned.1.call-start = ((), (), s32[]{:S(2)}) async-start(), calls=%async_computation.4 | async-start | bytes 1081344 | tf_op jit(solution)/shard_map/reduce_scatter | solution.py:66
  169.1 26.7 %copy-start = (f32[2048,1536]{1,0:T(8,128)S(1)}, f32[2048,1536]{1,0:T(8,128)}, u32[]{:S(2)}) copy-start(f32[2048,1536]{1,0:T(8,128)} %fusion.9) | copy-start | bytes 37748740
  195.8 6.9 copy-start.4
  210.6 8.8 %copy-start.3 = (f32[64,1536]{1,0:T(8,128)}, f32[64,1536]{1,0:T(8,128)S(1)}, u32[]{:S(2)}) copy-start(f32[64,1536]{1,0:T(8,128)S(1)} %get-tuple-element.10) | copy-start | bytes 1179652
  219.4 382.1 %reduce-scatter.5.cloned.1.call-start = ((), (), s32[]{:S(2)}) async-start(), calls=%async_computation.5 | async-start | bytes 25952256 | tf_op jit(solution)/shard_map/reduce_scatter | solution.py:67
  246.2 0.7 copy-start.5
  246.2 0.7 copy-start.6
  246.2 355.4 %copy-start.1 = (f32[64,3072]{1,0:T(8,128)S(1)}, f32[64,3072]{1,0:T(8,128)}, u32[]{:S(2)}) copy-start(f32[64,3072]{1,0:T(8,128)} %param.12) | copy-start | bytes 2359300
  246.2 355.4 %copy-start.2 = (f32[1,64,3072]{2,1,0:T(8,128)S(1)}, f32[1,64,3072]{2,1,0:T(8,128)}, u32[]{:S(2)}) copy-start(f32[1,64,3072]{2,1,0:T(8,128)} %param.13) | copy-start | bytes 2359300
  246.3 489.8 %all-reduce.3.cloned.1.call-start = ((), (), s32[]{:S(2)}) async-start(), calls=%async_computation.6 | async-start | bytes 1572864 | tf_op jit(solution)/shard_map/psum | solution.py:77
Sparse Core Ops, SparseCore 0:
  14.2 56.3 all-gather.2
  74.1 94.9 all-gather.4
  219.6 133.0 reduce-scatter.2
  360.1 241.4 reduce-scatter.4
  607.2 128.8 all-reduce.2

commit v2 on v1

v2 whole, which is shorter than its diff:
```python
import functools

import jax
import jax.numpy as jnp
from jax import lax
from jax.experimental import pallas as pl
from jax.experimental.pallas import tpu as pltpu
from jax.sharding import PartitionSpec as P

PASSES = 3
PENALTY = 5.0
PARTS = 3
GROUP = 4
VMEM = 127 * 512 * 1024


def hdot(left, right):
    return jnp.dot(left, right, preferred_element_type=jnp.float32, precision=lax.Precision.HIGHEST)


def nt_dot(left, right):
    return lax.dot_general(
        left, right, (((1,), (1,)), ((), ())), preferred_element_type=jnp.float32
    )


def orders_of(devices):
    high = []
    bit = devices // 2
    while bit > 1:
        high.append(bit)
        bit //= 2
    rolls = [0, len(high) - 1, len(high) // 2]
    orders = [high[k:] + high[:k] + [1] for k in rolls]
    return orders + [orders[0]]


def flip(me, bits):
    for bit in bits:
        me = me + bit - 2 * bit * ((me // bit) % 2)
    return me


def slots_of(target, me, order):
    apart = jnp.bitwise_xor(target, me)
    return sum(((apart // bit) % 2) * (1 << j) for j, bit in enumerate(order))


def enter(me, devices):
    barrier = pltpu.get_barrier_semaphore()
    bit = 1
    count = 0
    while bit < devices:
        pl.semaphore_signal(
            barrier,
            inc=1,
            device_id={"cells": flip(me, [bit])},
            device_id_type=pl.DeviceIdType.MESH,
        )
        bit *= 2
        count += 1
    pl.semaphore_wait(barrier, count)


def exchange(source, landing, sends, receives, part, stage, me, bit):
    return pltpu.make_async_remote_copy(
        src_ref=source,
        dst_ref=landing,
        send_sem=sends.at[part, stage],
        recv_sem=receives.at[part, stage],
        device_id={"cells": flip(me, [bit])},
        device_id_type=pl.DeviceIdType.MESH,
    )


def load_kernel(
    devices, q_ref, small_ref, x_ref, rel_ref, start_ref, h_ref, mean_ref, buf, side, acc, steps, sends, recvs
):
    me = lax.axis_index("cells")
    orders = orders_of(devices)
    stages = len(orders[0])
    factors, genes = q_ref.shape
    cells = x_ref.shape[0]
    width = genes // PARTS
    rows = GROUP * factors
    for p in range(PARTS):
        buf[p, 0] = q_ref[:, p * width : (p + 1) * width]
    side[0] = small_ref[...]
    acc[...] = jnp.zeros_like(acc)
    enter(me, devices)

    def copy(p, j):
        near, far = pl.ds(0, 1 << j), pl.ds(1 << j, 1 << j)
        if p == PARTS:
            return exchange(side.at[near], side.at[far], sends, recvs, p, j, me, orders[p][j])
        return exchange(buf.at[p, near], buf.at[p, far], sends, recvs, p, j, me, orders[p][j])

    def project(low, high):
        for p in range(PARTS):

            def one(g, carry, p=p):
                block = buf[p, pl.ds(g * GROUP, GROUP)].reshape(rows, width)
                product = nt_dot(block, x_ref[:, p * width : (p + 1) * width])
                slot = rel_ref[p : p + 1, :]
                total = acc[...]
                for i in range(GROUP):
                    total = total + jnp.where(
                        slot == g * GROUP + i, product[i * factors : (i + 1) * factors], 0.0
                    )
                acc[...] = total
                return carry

            lax.fori_loop(low // GROUP, high // GROUP, one, 0)

    for p in range(PARTS + 1):
        copy(p, 0).start()
    for j in range(stages):
        for p in range(PARTS + 1):
            copy(p, j).wait()
            if j + 1 < stages:
                copy(p, j + 1).start()
        if j == 1:
            project(0, 4)
        elif j > 1:
            project(1 << j, 2 << j)

    slot = rel_ref[PARTS : PARTS + 1, :]

    def step_of(s, carry):
        one = side[s][factors - 1 : factors, factors : factors + 1]
        mean_ref[...] = mean_ref[...] + side[s] * (1.0 / devices)
        steps[...] = steps[...] + jnp.where(slot == s, one, 0.0)
        return carry

    steps[...] = jnp.zeros_like(steps)
    mean_ref[...] = jnp.zeros_like(mean_ref)
    lax.fori_loop(0, devices, step_of, 0)
    acc[...] = acc[...] * steps[...]
    h_ref[...] = start_ref[...].astype(jnp.float32)
    for _ in range(PASSES):
        h = h_ref[...]
        high = h.astype(jnp.bfloat16)
        low = (h - high.astype(jnp.float32)).astype(jnp.bfloat16)
        h_cat = jnp.concatenate([high, high, low], axis=0)
        h_ref[...] = h + acc[...]

        def apply(g, carry, h_cat=h_cat):
            m = side[pl.ds(g * GROUP, GROUP)].reshape(rows, 2 * factors)[:, :factors]
            m_high = m.astype(jnp.bfloat16)
            m_low = (m - m_high.astype(jnp.float32)).astype(jnp.bfloat16)
            m_cat = jnp.concatenate([m_high, m_low, m_high], axis=1)
            product = jnp.dot(m_cat, h_cat, preferred_element_type=jnp.float32)
            total = h_ref[...]
            for i in range(GROUP):
                total = total - jnp.where(
                    slot == g * GROUP + i, product[i * factors : (i + 1) * factors], 0.0
                )
            h_ref[...] = total
            return carry

        lax.fori_loop(0, devices // GROUP, apply, 0)
        h_ref[...] = jnp.maximum(h_ref[...], 0.0)


def stat_kernel(
    devices, h_ref, x_ref, rel_ref, mean_ref, cross_ref, gram_ref, buf, land, side, side_land, held, arrived,
    sends, recvs
):
    me = lax.axis_index("cells")
    orders = orders_of(devices)
    stages = len(orders[0])
    factors, cells = h_ref.shape
    genes = x_ref.shape[1]
    width = genes // PARTS
    group = GROUP if devices <= 32 else GROUP // 2
    streamed = devices > 32
    enter(me, devices)

    def copy(p, j):
        far, landed = pl.ds(1 << j, 1 << j), pl.ds((1 << j) - 1, 1 << j)
        if p == PARTS:
            return exchange(side.at[far], side_land.at[landed], sends, recvs, p, j, me, orders[p][j])
        return exchange(buf.at[p, far], land.at[p, landed], sends, recvs, p, j, me, orders[p][j])

    def masked(p, g):
        slot = rel_ref[p : p + 1, :]
        h = h_ref[...]
        return jnp.concatenate(
            [jnp.where(slot == g * group + i, h, 0.0).astype(jnp.bfloat16) for i in range(group)],
            axis=0,
        )

    def fill(p, low, high):
        if streamed:
            fetch = pltpu.make_async_copy(x_ref.at[:, pl.ds(p * width, width)], held, arrived)
            fetch.start()
            fetch.wait()

        def one(g, carry):
            load = masked(p, g)
            columns = held[...] if streamed else x_ref[:, p * width : (p + 1) * width]
            product = jnp.dot(load, columns, preferred_element_type=jnp.float32)
            mass = jnp.sum(load.astype(jnp.float32), axis=1, keepdims=True)
            product = product - mass * mean_ref[:, p * width : (p + 1) * width]
            buf[p, pl.ds(g * group, group)] = product.astype(jnp.bfloat16).reshape(
                group, factors, width
            )
            return carry

        lax.fori_loop(low // group, high // group, one, 0)

    def fill_side(low, high):
        h = h_ref[...]
        h_high = h.astype(jnp.bfloat16)
        h_low = (h - h_high.astype(jnp.float32)).astype(jnp.bfloat16)
        both = jnp.concatenate([h_high, h_low], axis=0)
        slot = rel_ref[PARTS : PARTS + 1, :]

        def one(g, carry):
            load = masked(PARTS, g)
            product = nt_dot(load, both)
            mass = nt_dot(jnp.ones((16, cells), jnp.bfloat16), load)[0:8]
            for i in range(group):
                s = g * group + i
                here = jnp.sum(jnp.where(slot == s, 1.0, 0.0), axis=1, keepdims=True)
                side[s, 0:factors, :] = product[i * factors : (i + 1) * factors]
                side[s, factors : factors + 8, :] = jnp.concatenate(
                    [
                        mass[:, i * factors : (i + 1) * factors],
                        jnp.broadcast_to(here, (8, factors)),
                    ],
                    axis=1,
                )
            return carry

        lax.fori_loop(low // group, high // group, one, 0)

    def gather_in(p, j, low, high):
        def one(s, carry):
            if p == PARTS:
                side[s] = side[s] + side_land[(1 << j) - 1 + s]
            else:
                buf[p, s] = (
                    buf[p, s].astype(jnp.float32) + land[p, (1 << j) - 1 + s].astype(jnp.float32)
                ).astype(jnp.bfloat16)
            return carry

        lax.fori_loop(low, high, one, 0)

    half = devices // 2
    for p in range(PARTS):
        fill(p, half, devices)
        copy(p, stages - 1).start()
    fill_side(half, devices)
    copy(PARTS, stages - 1).start()
    for p in range(PARTS):
        fill(p, 0, half)
    fill_side(0, half)
    for j in range(stages - 1, 0, -1):
        for p in range(PARTS + 1):
            copy(p, j).wait()
            gather_in(p, j, 1 << (j - 1), 1 << j)
            copy(p, j - 1).start()
        for p in range(PARTS + 1):
            gather_in(p, j, 0, 1 << (j - 1))
    for p in range(PARTS):
        copy(p, 0).wait()
        cross_ref[:, p * width : (p + 1) * width] = buf[p, 0].astype(jnp.float32) + land[
            p, 0
        ].astype(jnp.float32)
    copy(PARTS, 0).wait()
    gram_ref[...] = side[0] + side_land[0]


def sum_kernel(devices, x_ref, out_ref, buf, land, spread, sends, recvs):
    me = lax.axis_index("cells")
    order = orders_of(devices)[0]
    stages = len(order)

    def block(r):
        return flip(me, [bit for j, bit in enumerate(order) if (r >> j) % 2])

    for r in range(devices):
        buf[r] = x_ref[block(r)]
    enter(me, devices)

    def inward(j):
        far = pl.ds(1 << j, 1 << j)
        return exchange(buf.at[far], land.at[far], sends, recvs, 0, j, me, order[j])

    def outward(j):
        near, far = pl.ds(0, 1 << j), pl.ds(1 << j, 1 << j)
        return exchange(spread.at[near], spread.at[far], sends, recvs, 1, j, me, order[j])

    for j in range(stages - 1, -1, -1):
        inward(j).start()
        inward(j).wait()
        near = pl.ds(0, 1 << j)
        buf[near] = buf[near] + land[pl.ds(1 << j, 1 << j)]
    spread[0] = buf[0]
    for j in range(stages):
        outward(j).start()
        outward(j).wait()
    for r in range(devices):
        out_ref[block(r)] = spread[r]


def in_vmem(count):
    return [pl.BlockSpec(memory_space=pltpu.VMEM)] * count


def params(number):
    return pltpu.CompilerParams(
        collective_id=number, has_side_effects=True, vmem_limit_bytes=VMEM
    )


def body(expression, dataset_ids, owner_map, atlas_sizes, loadings, shared, specific):
    devices = lax.axis_size("cells")
    me = lax.axis_index("cells")
    cells, genes = expression.shape
    factors = shared.shape[0]
    width = genes // PARTS
    orders = orders_of(devices)
    stages = len(orders[0])
    v = specific[0]
    q = shared + v
    curvature = hdot(q, q.T) + PENALTY * hdot(v, v.T)
    step = 1.0 / jnp.max(jnp.sum(jnp.abs(curvature), axis=1))
    lines = genes // factors
    typical = jnp.mean(expression[: cells // 6].astype(jnp.float32), axis=0)
    extra = jnp.concatenate(
        [typical.reshape(lines, factors), jnp.full((factors - lines, factors), step)], axis=0
    )
    small = jnp.concatenate([curvature * step, extra], axis=1)
    ids = dataset_ids[:, 0]
    chosen = ids[None, :] == jnp.arange(owner_map.shape[0], dtype=jnp.int32)[:, None]
    target = jnp.sum(jnp.where(chosen, owner_map[:, None], 0), axis=0)
    rel = jnp.stack([slots_of(target, me, order) for order in orders] * 2, axis=0)
    semaphores = [
        pltpu.SemaphoreType.DMA((PARTS + 1, stages)),
        pltpu.SemaphoreType.DMA((PARTS + 1, stages)),
    ]
    h, mean = pl.pallas_call(
        functools.partial(load_kernel, devices),
        out_shape=(
            jax.ShapeDtypeStruct((factors, cells), jnp.float32),
            jax.ShapeDtypeStruct((factors, 2 * factors), jnp.float32),
        ),
        in_specs=in_vmem(5),
        out_specs=tuple(in_vmem(2)),
        scratch_shapes=[
            pltpu.VMEM((PARTS, devices, factors, width), jnp.bfloat16),
            pltpu.VMEM((devices, factors, 2 * factors), jnp.float32),
            pltpu.VMEM((factors, cells), jnp.float32),
            pltpu.VMEM((1, cells), jnp.float32),
        ]
        + semaphores,
        compiler_params=params(0),
        name="load_kernel",
    )(q.astype(jnp.bfloat16), small, expression, rel, loadings)
    center = mean[:lines, factors:].reshape(1, genes)
    cross, gram2 = pl.pallas_call(
        functools.partial(stat_kernel, devices),
        out_shape=(
            jax.ShapeDtypeStruct((factors, genes), jnp.float32),
            jax.ShapeDtypeStruct((factors + 8, 2 * factors), jnp.float32),
        ),
        in_specs=in_vmem(1)
        + [pl.BlockSpec(memory_space=pl.ANY if devices > 32 else pltpu.VMEM)]
        + in_vmem(2),
        out_specs=tuple(in_vmem(2)),
        scratch_shapes=[
            pltpu.VMEM((PARTS, devices, factors, width), jnp.bfloat16),
            pltpu.VMEM((PARTS, devices - 1, factors, width), jnp.bfloat16),
            pltpu.VMEM((devices, factors + 8, 2 * factors), jnp.float32),
            pltpu.VMEM((devices - 1, factors + 8, 2 * factors), jnp.float32),
            pltpu.VMEM((cells, width) if devices > 32 else (16, 128), jnp.bfloat16),
            pltpu.SemaphoreType.DMA,
        ]
        + semaphores,
        compiler_params=params(1),
        name="stat_kernel",
    )(h, expression, rel, center)
    count = gram2[factors, factors]
    cross = cross + gram2[factors, :factors][:, None] * center
    mixed = gram2[:factors, factors:]
    gram = (gram2[:factors, :factors] + mixed + mixed.T) / count
    weight = jnp.sum(jnp.where(owner_map == me, atlas_sizes, 0)).astype(jnp.float32) / 65536.0
    gradient = hdot(gram, q) - cross / count
    bound = jnp.max(jnp.sum(gram, axis=1))
    new_specific = jnp.maximum(
        v - (gradient + PENALTY * hdot(gram, v)) / ((1.0 + PENALTY) * bound + 1e-06), 0.0
    )
    share = factors * genes // devices // 8
    terms = jnp.concatenate(
        [
            (weight * gradient).reshape(devices, 8, share),
            jnp.full((devices, 8, 128), weight * bound),
        ],
        axis=2,
    )
    wide = share + 128
    totals = pl.pallas_call(
        functools.partial(sum_kernel, devices),
        out_shape=jax.ShapeDtypeStruct((devices, 8, wide), jnp.float32),
        in_specs=in_vmem(1),
        out_specs=pl.BlockSpec(memory_space=pltpu.VMEM),
        scratch_shapes=[pltpu.VMEM((devices, 8, wide), jnp.float32)] * 3
        + [pltpu.SemaphoreType.DMA((2, stages)), pltpu.SemaphoreType.DMA((2, stages))],
        compiler_params=params(2),
        name="sum_kernel",
    )(terms)
    grad_total = totals[:, :, :share].reshape(factors, genes)
    shared_out = jnp.maximum(shared - grad_total / totals[0, 0, share], 0.0)
    return (h, shared_out, new_specific[None])


def solution(mesh):
    placed = (
        P(("groups", "cells"), None),
        P(("groups", "cells"), None),
        P("groups"),
        P("groups"),
        P(None, ("groups", "cells")),
        P("groups", None),
        P(("groups", "cells"), None, None),
    )
    return jax.shard_map(
        body,
        mesh=mesh,
        in_specs=placed,
        out_specs=(
            P(None, ("groups", "cells")),
            P("groups", None),
            P(("groups", "cells"), None, None),
        ),
        check_vma=False,
    )
```

time: 746 us -> 295 us (0.40)
  waiting for transfers between devices: 539 us -> 0 us
  Pallas kernels: 0 us -> 257 us
  blocking collectives: 79.2 us -> 0 us
  matrix products: 79.4 us -> 11.3 us
  other arithmetic: 27.2 us -> 13.5 us
  between operations: 16.6 us -> 3.4 us
    reduce_scatter x2 -> x0, waiting for transfers between devices: 312 us -> none  [the longest x1 246 us: body(): lax.psum_scatter(cross_part, 'cells', scatter_dimension=0, tiled=True)]
    pallas_call x0 -> x3, Pallas kernels: none -> 257 us  [the longest x1 111 us: body(): pl.pallas_call(functools.partial(load_kernel, devices), out_shape=(jax.Sh...]
    all_gather x2 -> x0, waiting for transfers between devices: 141 us -> none  [the longest x1 89.3 us: body(): qb_all = lax.all_gather(q.astype(jnp.bfloat16), 'cells', axis=0, tiled=True)]
    psum x1 -> x0, waiting for transfers between devices: 86.7 us -> none  [body(): lax.psum((weight * gradient, weight * bound), 'cells')]
    psum x2 -> x0, blocking collectives: 79.2 us -> none  [the longest x1 40.5 us: body(): lax.psum((weight * gradient, weight * bound), 'cells')]
    dot_general x6 -> x0, matrix products: 69.1 us -> none  [the longest x1 26.7 us: body(): cross_part = jnp.dot(masked, expression, preferred_element_type=jnp.float32)]
    reduce_sum x6 -> x2, other arithmetic: 12.2 us -> 2.42 us  [the longest x1 1.67 us: body(): typical = jnp.mean(expression[:cells // 6].astype(jnp.float32), axis=0)]
  transfers between devices with their start and end apart: 5 -> 0, of which waited for: 5 -> 0; matrix products, arithmetic and copies ran while one was open for 6% -> 0% of each run, Pallas kernels for 0% -> 0%
where the time goes in v2:
time: 295 us; the launch traced here: 294 us
  Pallas kernels  257 us (87%)
  other arithmetic  13.5 us (5%)
  matrix products  11.3 us (4%)
  local copies, waits for them, and re-layouts  9.46 us (3%)
  between operations  3.4 us (1%)
    pallas_call x1, Pallas kernels, body(): pl.pallas_call(functools.partial(load_kernel, devices), out_shape=(jax.Sh...  111 us
    pallas_call x1, Pallas kernels, body(): pl.pallas_call(functools.partial(stat_kernel, devices), out_shape=(jax.Sh...  106 us
    pallas_call x1, Pallas kernels, body(): pl.pallas_call(functools.partial(sum_kernel, devices), out_shape=jax.Shap...  39.5 us
    dot_general x4, matrix products, hdot(): jnp.dot(left, right, preferred_element_type=jnp.float32, precision=lax.Pr...  11.3 us

profile of v2, /device:TPU:0, one launch (start us, length us, event | category | flops | bytes accessed | tf_op | source)
XLA Modules:
  0.0 294.3 jit_solution(8974187502867150890)
XLA Ops:
  0.6 0.7 reduce
  1.4 0.8 select_reduce_fusion
  2.1 0.2 add_add_fusion
  2.3 0.7 stack.2.rel_ref
  3.0 2.7 fusion.16
  5.7 2.3 abs_reduce_fusion
  8.0 0.6 reduce_max.18
  9.3 1.7 convert_reduce_fusion
  11.1 0.7 select_maximum_fusion.small_ref
  11.8 2.2 fusion.17.q_ref
  14.0 111.3 %load_kernel.1 = (f32[64,1536]{1,0:T(8,128)}, f32[64,128]{1,0:T(8,128)}) custom-call(bf16[64,3072]{1,0:T(8,128)(2,1)} %fusion.17.q_ref, f32[64,128]{1,0:T(8,128)} %select_maximum_fusion.small_ref, bf16[1536,3072]{1,0:T(8,128)(2,1)} %x_ref.3, s32[8,1536]{1,0:T(8,128)} %stack.2.rel_ref, bf16[64,1536]{1,0:T(8,128)(2,1)} %start_ref.1), custom_call_target="tpu_custom_call" | custom-call | tf_op jit(solution)/shard_map/load_kernel/pallas_call | solution.py:344
  125.3 0.8 slice.25
  126.1 0.7 reshape.392.mean_ref
  126.8 105.8 %stat_kernel.1 = (f32[64,3072]{1,0:T(8,128)}, f32[72,128]{1,0:T(8,128)}) custom-call(f32[64,1536]{1,0:T(8,128)} %get-tuple-element.23.h_ref, bf16[1536,3072]{1,0:T(8,128)(2,1)} %x_ref.3, s32[8,1536]{1,0:T(8,128)} %stack.2.rel_ref, f32[1,3072]{1,0:T(1,128)} %reshape.392.mean_ref), custom_call_target="tpu_custom_call" | custom-call | tf_op jit(solution)/shard_map/stat_kernel/pallas_call | solution.py:363
  232.6 1.3 slice.28
  233.9 0.9 copy.12
  234.7 0.8 slice.27
  235.6 0.1 copy.13
  235.6 1.5 fusion.18
  237.2 0.7 slice_bitcast_fusion
  237.9 0.6 fusion.15
  239.2 3.1 %broadcast_multiply_fusion = (f32[64,3072]{1,0:T(8,128)S(1)}, f32[64,3072]{1,0:T(8,128)S(1)}) fusion(f32[]{:T(128)S(6)} %div.129, f32[]{:T(128)} %bitcast.2, f32[64,3072]{1,0:T(8,128)} %get-tuple-element.10, f32[3072]{0:T(1024)S(1)} %mul.175, f32[64]{0:T(128)S(1)} %slice_bitcast_fusion, f32[64,64]{0,1:T(8,128)S(1)} %get-tuple-element.12, ...), kind=kOutput, calls=%fused_computation.15 | convolution fusion | flops 152174592 | bytes 3961096 | tf_op jit(solution)/shard_map/dot_general | solution.py:18
  242.4 0.6 reduce_max.19
  243.6 3.2 %fusion.4 = f32[1,64,3072]{2,1,0:T(8,128)} fusion(f32[64,3072]{1,0:T(8,128)S(1)} %get-tuple-element.19, f32[64,64]{0,1:T(8,128)S(1)} %get-tuple-element.12, f32[1,64,3072]{2,1,0:T(8,128)} %param.13, f32[]{:T(128)S(6)} %add.367), kind=kOutput, calls=%fused_computation.6 | convolution fusion | flops 151977984 | bytes 2375684 | tf_op jit(solution)/shard_map/dot_general | solution.py:18
  246.8 0.2 reshape.393
  247.7 1.0 concatenate.11.x_ref
  248.7 39.5 %sum_kernel.1 = f32[32,8,896]{2,1,0:T(8,128)} custom-call(f32[32,8,896]{2,1,0:T(8,128)} %concatenate.11.x_ref), custom_call_target="tpu_custom_call" | custom-call | tf_op jit(solution)/shard_map/sum_kernel/pallas_call | solution.py:404
  288.2 1.2 slice.31
  289.4 1.8 slice_divide_fusion
  291.2 0.2 div.136
  291.5 2.1 subtract_maximum_fusion
  293.6 0.7 copy.15
  (11 shorter events, 0.2 us)
Async XLA Ops:
  14.0 223.9 %copy-start.1 = (s32[32]{0:T(128)S(1)}, s32[32]{0:T(128)}, u32[]{:S(2)}) copy-start(s32[32]{0:T(128)} %param.9) | copy-start | bytes 388
  14.0 223.9 %copy-start.2 = (s32[32]{0:T(128)S(1)}, s32[32]{0:T(128)}, u32[]{:S(2)}) copy-start(s32[32]{0:T(128)} %param.10) | copy-start | bytes 388
  232.6 61.0 %copy-start = (f32[64,1536]{1,0:T(8,128)S(1)}, f32[64,1536]{1,0:T(8,128)}, u32[]{:S(2)}) copy-start(f32[64,1536]{1,0:T(8,128)} %get-tuple-element.23.h_ref) | copy-start | bytes 1179652
